TPU v7x, 32 devices: a whole 2x2x4 slice. The times are simulated.
32 devices in a mesh: seg: 8 (over y, x, core), row: 4 (over z).
Axes of the slice: x: 2, y: 2, z: 4, core: 2. Of those that a mesh axis runs over, the one named last changes fastest.
Arguments:
- left_env: bfloat16 [8, 512, 12, 512], P('seg', 'row'), may hold values from -4 to 4, as said below
- right_env: bfloat16 [8, 512, 12, 512], P('seg'), may hold values from -4 to 4, as said below
- site_operator: bfloat16 [4, 12, 12, 4], replicated, may hold values from -1 to 2, as said below
- start_vector: float32 [8, 512, 4, 512], P('seg', 'row'), may hold values from -6 to 6
Outputs:
- last_vector: float32 [8, 512, 4, 512], P('seg', 'row')
- alpha_values: float32 [8, 2], P('seg')
- beta_values: float32 [8, 2], P('seg')
Inputs may be any that keep to these rules, and one draw needn't show every extreme that they name: left_env[i, a, w, c] = left_env[i, c, w, a]. right_env[i, a, w, c] = right_env[i, c, w, a]. site_operator[s, v, w, r] = site_operator[r, v, w, s].
All inputs are finite; a program needn't handle non-finite values.
Results may differ from a plain program's by a relative error of at most 0.0076.
Values may be sent and summed in bfloat16 or wider, within the bound.
A program may use at most 128 MiB of HBM per device.

v0:
```python
import jax
import jax.numpy as jnp
from jax import lax
from jax.sharding import PartitionSpec as P

ITERS = 2


def passed_along(value, axis, steps):
    count = lax.axis_size(axis)
    initial, last = (max(0, -steps), min(count, count - steps))
    return lax.ppermute(value, axis, [(source, source + steps) for source in range(initial, last)])


def local(left_env, right_env, site_operator, start_vector):
    rows_here = left_env.shape[1]
    channels = left_env.shape[2]
    bond_width = left_env.shape[3]
    physical = site_operator.shape[0]
    entries = float(bond_width * physical * bond_width)
    left_local = left_env[0]
    operator_mat = site_operator.reshape(physical * channels, channels * physical)
    last_segment = lax.axis_index("seg") == lax.axis_size("seg") - 1
    received = passed_along(right_env, "seg", -1)
    right_used = jnp.where(last_segment, right_env, received)
    right_mat = right_used[0].reshape(bond_width, channels * bond_width)
    start_local = start_vector[0]
    norm_start = lax.psum(jnp.sum(start_local * start_local), "row") / entries
    current = start_local / jnp.sqrt(norm_start + 1e-06)
    previous = jnp.zeros_like(current)
    beta_prev = jnp.zeros((), jnp.float32)
    alpha_list = []
    beta_list = []
    for step_index in range(ITERS):
        lowered = current.astype(jnp.bfloat16)
        gathered = lax.all_gather(lowered, "row", axis=0, tiled=True)
        contracted = jnp.dot(
            left_local.reshape(rows_here * channels, bond_width),
            gathered.reshape(bond_width, physical * bond_width),
            preferred_element_type=jnp.float32,
        )
        contracted = contracted.astype(jnp.bfloat16).reshape(
            rows_here, channels * physical, bond_width
        )
        mixed = jnp.einsum(
            "ik,akb->aib", operator_mat, contracted, preferred_element_type=jnp.float32
        )
        mixed = mixed.astype(jnp.bfloat16).reshape(rows_here, physical, channels * bond_width)
        image = jnp.einsum("asc,bc->asb", mixed, right_mat, preferred_element_type=jnp.float32)
        image_image, image_curr, image_prev, curr_curr, prev_prev, curr_prev = lax.psum(
            (
                jnp.sum(image * image),
                jnp.sum(image * current),
                jnp.sum(image * previous),
                jnp.sum(current * current),
                jnp.sum(previous * previous),
                jnp.sum(current * previous),
            ),
            "row",
        )
        alpha = image_curr / entries
        norm_sq = (
            image_image
            - 2.0 * alpha * image_curr
            - 2.0 * beta_prev * image_prev
            + alpha * alpha * curr_curr
            + beta_prev * beta_prev * prev_prev
            + 2.0 * alpha * beta_prev * curr_prev
        ) / entries
        residual_vec = image - alpha * current - beta_prev * previous
        beta_next = jnp.sqrt(norm_sq + 1e-06)
        previous = current
        current = residual_vec / beta_next
        beta_prev = beta_next
        alpha_list.append(alpha)
        beta_list.append(beta_next)
    alpha_values = jnp.stack(alpha_list).reshape(1, ITERS)
    beta_values = jnp.stack(beta_list).reshape(1, ITERS)
    return (current[None], alpha_values, beta_values)


def solution(mesh):
    placed = (
        P("seg", "row", None, None),
        P("seg", None, None, None),
        P(),
        P("seg", "row", None, None),
    )
    return jax.shard_map(
        local,
        mesh=mesh,
        in_specs=placed,
        out_specs=(P("seg", "row", None, None), P("seg", None), P("seg", None)),
        check_vma=False,
    )
```

profile of v0, /device:TPU:0, one launch (start us, length us, event | category | flops | bytes accessed | tf_op | source)
XLA Modules:
  0.0 300.8 jit_solution(16806568525329012419)
XLA Ops:
  7.2 8.7 %copy.18 = bf16[1,512,12,512]{1,3,2,0:T(8,128)(2,1)} copy(bf16[1,512,12,512]{3,1,2,0:T(8,128)(2,1)} %param.5) | data formatting | bytes 12582912 | tf_op args[1]
  15.9 1.4 collective-permute-start
  18.5 14.0 %psum.87 = f32[]{:T(128)} all-reduce(f32[]{:T(128)} %multiply_reduce_fusion.5), channel_id=1, replica_groups=mesh['seg'=8,'row'=4] {'row'}, use_global_device_ids=true, to_apply=%region_1.2 | all-reduce | flops 1 | bytes 8 | tf_op jit(solution)/shard_map/psum | solution.py:28
  34.4 2.3 copy.13
  38.4 41.6 %all-gather.3.cloned.1.call-done = bf16[512,4,512]{2,0,1:T(8,128)(2,1)} async-done(((bf16[128,4,512]{2,0,1:T(8,128)(2,1)}), bf16[512,4,512]{2,0,1:T(8,128)(2,1)}) %all-gather.3.cloned.1.call-update) | async-done | bytes 2097168 | tf_op jit(solution)/shard_map/all_gather | solution.py:36
  80.0 2.8 copy.12
  82.8 6.8 %fusion = bf16[1536,2048]{0,1:T(8,128)(2,1)} fusion(bf16[512,2048]{0,1:T(8,128)(2,1)S(1)} %bitcast.73, bf16[1536,512]{1,0:T(8,128)(2,1)} %reshape_squeeze.7), kind=kOutput, calls=%fused_computation.2 | convolution fusion | flops 3224371200 | bytes 9961472 | tf_op jit(solution)/shard_map/dot_general | solution.py:37
  89.6 8.6 %copy.14 = bf16[1536,2048]{1,0:T(8,128)(2,1)} copy(bf16[1536,2048]{0,1:T(8,128)(2,1)} %fusion) | data formatting | bytes 12582912 | tf_op jit(solution)/shard_map/convert_element_type | solution.py:42
  98.2 10.7 %reshape.37 = bf16[128,48,512]{2,1,0:T(8,128)(2,1)} reshape(bf16[1536,2048]{1,0:T(8,128)(2,1)} %copy.14) | data formatting | bytes 12582912 | tf_op jit(solution)/shard_map/reshape | solution.py:42
  108.9 7.3 %convert_bitcast_fusion.1 = bf16[128,48,512]{2,1,0:T(8,128)(2,1)} fusion(bf16[128,48,512]{2,1,0:T(8,128)(2,1)} %reshape.37, bf16[48,48]{0,1:T(8,128)(2,1)S(1)} %reshape.38), kind=kOutput, calls=%fused_computation.9 | convolution fusion | flops 305135616 | bytes 12587520 | tf_op jit(solution)/shard_map/ik,akb->aib/dot_general | solution.py:45
  116.2 13.6 %reshape.39 = bf16[128,4,6144]{2,1,0:T(4,128)(2,1)} reshape(bf16[128,48,512]{2,1,0:T(8,128)(2,1)} %convert_bitcast_fusion.1) | data formatting | bytes 12582912 | tf_op jit(solution)/shard_map/reshape | solution.py:48
  129.8 6.1 %broadcast_select_fusion = bf16[1,512,12,512]{1,3,2,0:T(8,128)(2,1)} fusion(bf16[1,512,12,512]{1,3,2,0:T(8,128)(2,1)} %copy.18, bf16[1,512,12,512]{1,3,2,0:T(8,128)(2,1)} %collective-permute-done, pred[]{:T(512)S(6)} %eq.3), kind=kLoop, calls=%fused_computation.10 | loop fusion | flops 3145728 | bytes 18874368 | tf_op jit(solution)/shard_map/jit(_where)/select_n | solution.py:25
  135.9 11.5 %fusion.10 = (f32[]{:T(128)}, f32[]{:T(128)}, f32[]{:T(128)}, f32[]{:T(128)}, f32[]{:T(128)}, /*index=5*/f32[128,4,512]{2,0,1:T(8,128)S(1)}) fusion(f32[]{:T(128)S(6)} %sqrt.9, f32[1,128,4,512]{3,2,1,0:T(4,128)S(1)} %copy-done, bf16[512,6144,1]{0,1,2:T(8,128)(2,1)} %bitcast.70, bf16[128,4,6144]{2,1,0:T(4,128)(2,1)} %reshape.39), kind=kOutput, calls=%fused_computation.23 | convolution fusion | flops 3224109056 | bytes 14680088 | tf_op jit(solution)/shard_map/asc,bc->asb/dot_general | solution.py:49
  147.4 10.9 %all-reduce.1 = (f32[]{:T(128)}, f32[]{:T(128)}, f32[]{:T(128)}, f32[]{:T(128)}, f32[]{:T(128)}, /*index=5*/f32[]{:T(128)}) all-reduce(f32[]{:T(128)} %get-tuple-element.18, f32[]{:T(128)} %get-tuple-element.16, f32[]{:T(128)} %get-tuple-element.17, f32[]{:T(128)} %get-tuple-element.15, ...), channel_id=1, replica_groups=mesh['seg'=8,'row'=4] {'row'}, use_global_device_ids=true, to_apply=%region_5.6 | all-reduce | flops 6 | bytes 48 | tf_op jit(solution)/shard_map/psum | solution.py:50
  167.3 43.9 %all-gather.5.cloned.1.call-done = bf16[512,4,512]{2,0,1:T(8,128)(2,1)} async-done(((bf16[128,4,512]{2,0,1:T(8,128)(2,1)}), bf16[512,4,512]{2,0,1:T(8,128)(2,1)}) %all-gather.5.cloned.1.call-update) | async-done | bytes 2097168 | tf_op jit(solution)/shard_map/all_gather | solution.py:36
  211.2 4.2 %copy.21 = bf16[512,4,512]{0,2,1:T(8,128)(2,1)} copy(bf16[512,4,512]{2,0,1:T(8,128)(2,1)} %all-gather.5.cloned.1.call-done) | data formatting | bytes 4194304 | tf_op jit(solution)/shard_map/all_gather | solution.py:36
  215.3 8.2 %fusion.1 = bf16[1536,2048]{0,1:T(8,128)(2,1)} fusion(bf16[512,2048]{0,1:T(8,128)(2,1)} %bitcast.72, bf16[1536,512]{1,0:T(8,128)(2,1)} %reshape_squeeze.7), kind=kOutput, calls=%fused_computation.3 | convolution fusion | flops 3224371200 | bytes 9961472 | tf_op jit(solution)/shard_map/dot_general | solution.py:37
  223.5 8.6 %copy.22 = bf16[1536,2048]{1,0:T(8,128)(2,1)} copy(bf16[1536,2048]{0,1:T(8,128)(2,1)} %fusion.1) | data formatting | bytes 12582912 | tf_op jit(solution)/shard_map/convert_element_type | solution.py:42
  232.1 10.7 %reshape.41 = bf16[128,48,512]{2,1,0:T(8,128)(2,1)} reshape(bf16[1536,2048]{1,0:T(8,128)(2,1)} %copy.22) | data formatting | bytes 12582912 | tf_op jit(solution)/shard_map/reshape | solution.py:42
  242.8 7.2 %convert_bitcast_fusion = bf16[128,48,512]{2,1,0:T(8,128)(2,1)} fusion(bf16[128,48,512]{2,1,0:T(8,128)(2,1)} %reshape.41, bf16[48,48]{0,1:T(8,128)(2,1)S(1)} %reshape.38), kind=kOutput, calls=%fused_computation.8 | convolution fusion | flops 305135616 | bytes 12587520 | tf_op jit(solution)/shard_map/ik,akb->aib/dot_general | solution.py:45
  250.0 13.6 %reshape.42 = bf16[128,4,6144]{2,1,0:T(4,128)(2,1)} reshape(bf16[128,48,512]{2,1,0:T(8,128)(2,1)} %convert_bitcast_fusion) | data formatting | bytes 12582912 | tf_op jit(solution)/shard_map/reshape | solution.py:48
  263.6 11.5 %fusion.15 = (f32[]{:T(128)}, f32[]{:T(128)}, f32[]{:T(128)}, f32[]{:T(128)}, f32[]{:T(128)}, /*index=5*/f32[128,4,512]{2,0,1:T(8,128)S(1)}) fusion(f32[128,4,512]{2,0,1:T(8,128)S(1)} %get-tuple-element.31, f32[]{:T(128)S(6)} %sqrt.9, f32[1,128,4,512]{3,2,1,0:T(4,128)S(1)} %copy-done, bf16[512,6144,1]{0,1,2:T(8,128)(2,1)} %bitcast.71, ...), kind=kOutput, calls=%fused_computation.28 | convolution fusion | flops 3224109056 | bytes 15728664 | tf_op jit(solution)/shard_map/asc,bc->asb/dot_general | solution.py:49
  275.1 10.2 %all-reduce = (f32[]{:T(128)}, f32[]{:T(128)}, f32[]{:T(128)}, f32[]{:T(128)}, f32[]{:T(128)}) all-reduce(f32[]{:T(128)} %get-tuple-element.12, f32[]{:T(128)} %get-tuple-element.11, f32[]{:T(128)} %get-tuple-element.10, f32[]{:T(128)} %get-tuple-element.13, f32[]{:T(128)} %get-tuple-element.9), channel_id=1, replica_groups=mesh['seg'=8,'row'=4] {'row'}, use_global_device_ids=true, to_apply=%region_16.17 | all-reduce | flops 5 | bytes 40 | tf_op jit(solution)/shard_map/psum | solution.py:50
  291.7 1.6 copy.26
  (17 shorter events, 6.3 us)
Async XLA Ops:
  7.2 10.2 %copy-start = (f32[1,128,4,512]{3,2,1,0:T(4,128)S(1)}, f32[1,128,4,512]{3,2,1,0:T(4,128)}, u32[]{:S(2)}) copy-start(f32[1,128,4,512]{3,2,1,0:T(4,128)} %param.7) | copy-start | bytes 3145732
  7.2 72.9 %all-gather.3.cloned.1.call-start = ((), (), s32[]{:S(2)}) async-start(), calls=%async_computation | async-start | bytes 2621440 | tf_op jit(solution)/shard_map/all_gather | solution.py:36
  15.9 22.1 %copy-start.1 = (bf16[4,12,12,4]{2,3,1,0:T(4,128)(2,1)S(1)}, bf16[4,12,12,4]{2,3,1,0:T(4,128)(2,1)}, u32[]{:S(2)}) copy-start(bf16[4,12,12,4]{2,3,1,0:T(4,128)(2,1)} %param.6) | copy-start | bytes 13828
  15.9 113.9 %collective-permute-start = (bf16[1,512,12,512]{1,3,2,0:T(8,128)(2,1)}, bf16[1,512,12,512]{1,3,2,0:T(8,128)(2,1)}, u32[]{:S(2)}, u32[]{:S(2)}) collective-permute-start(bf16[1,512,12,512]{1,3,2,0:T(8,128)(2,1)} %copy.18), channel_id=1, source_target_pairs={{4,0},{8,4},{12,8},{16,12},{20,16},{24,20},{28,24},{5,1},{9,5},{13... | collective-permute-start | bytes 18874376 | tf_op jit(solution)/shard_map/ppermute | solution.py:12
  34.3 176.8 %all-gather.5.cloned.1.call-start = ((), (), s32[]{:S(2)}) async-start(), calls=%async_computation.1 | async-start | bytes 2621440 | tf_op jit(solution)/shard_map/all_gather | solution.py:36
Sparse Core Ops, SparseCore 0:
  34.4 45.5 all-gather.2
  166.7 44.3 all-gather.4
where the time goes:
time: 303 us; the launch traced here: 301 us
  local copies, waits for them, and re-layouts  87.1 us (29%)
  waiting for transfers between devices  85.5 us (28%)
  matrix products  52.4 us (17%)
  blocking collectives  35.1 us (12%)
  between operations  28.4 us (9%)
  other arithmetic  10.6 us (3%)
    all_gather x2, waiting for transfers between devices, local(): gathered = lax.all_gather(lowered, 'row', axis=0, tiled=True)  85.5 us
    reshape x2, local copies, waits for them, and re-layouts, local(): mixed.astype(jnp.bfloat16)  27.2 us
    dot_general x2, matrix products, local(): jnp.einsum('asc,bc->asb', mixed, right_mat, preferred_element_type=jnp.fl...  22.9 us
    reshape x2, local copies, waits for them, and re-layouts, local(): contracted.astype(jnp.bfloat16)  21.4 us
    psum x2, blocking collectives, local(): lax.psum((jnp.sum(image * image), jnp.sum(image * current), jnp.sum(image...  21.1 us
    convert_element_type x2, local copies, waits for them, and re-layouts, local(): contracted.astype(jnp.bfloat16)  17.2 us
    dot_general x2, matrix products, local(): jnp.dot(left_local.reshape(rows_here * channels, bond_width), gathered.re...  14.9 us
    dot_general x2, matrix products, local(): jnp.einsum('ik,akb->aib', operator_mat, contracted, preferred_element_typ...  14.6 us
  transfers between devices with their start and end apart: 3, of which 2 were waited for; matrix products, arithmetic and copies ran while one was open for 19% of the time, Pallas kernels for 0%

commit v1 on v0

--- a/solution.py
+++ b/solution.py
@@ -33,7 +33,14 @@
     beta_list = []
     for step_index in range(ITERS):
         lowered = current.astype(jnp.bfloat16)
-        gathered = lax.all_gather(lowered, "row", axis=0, tiled=True)
+        ring = [lowered]
+        for hop in range(3):
+            ring.append(lax.ppermute(ring[-1], "row", [(dev, (dev + 1) % 4) for dev in range(4)]))
+        gathered = jnp.roll(
+            jnp.concatenate(ring[::-1], axis=0),
+            (lax.axis_index("row") + 1) * ring[0].shape[0],
+            axis=0,
+        )
         contracted = jnp.dot(
             left_local.reshape(rows_here * channels, bond_width),
             gathered.reshape(bond_width, physical * bond_width),

time: 303 us -> 290 us (0.957)
  waiting for transfers between devices: 85.5 us -> 69.6 us
  between operations: 28.4 us -> 15.1 us
  other arithmetic: 10.6 us -> 19.1 us
  starting transfers between devices: 1.49 us -> 6.5 us
    all_gather x2 -> x0, waiting for transfers between devices: 85.5 us -> none  [local(): gathered = lax.all_gather(lowered, 'row', axis=0, tiled=True)]
    ppermute x0 -> x6, waiting for transfers between devices: none -> 69.6 us  [local(): lax.ppermute(ring[-1], 'row', [(dev, (dev + 1) % 4) for dev in range(4)])]
    concatenate x0 -> x2, other arithmetic: none -> 9.15 us  [local(): jnp.roll(jnp.concatenate(ring[::-1], axis=0), (lax.axis_index('row') + 1)...]
    all_gather x2 -> x0, local copies, waits for them, and re-layouts: 6.95 us -> none  [local(): gathered = lax.all_gather(lowered, 'row', axis=0, tiled=True)]
    ppermute x0 -> x6, starting transfers between devices: none -> 5.22 us  [local(): lax.ppermute(ring[-1], 'row', [(dev, (dev + 1) % 4) for dev in range(4)])]
    dynamic_slice x0 -> x2, local copies, waits for them, and re-layouts: none -> 4.82 us  [local(): jnp.roll(jnp.concatenate(ring[::-1], axis=0), (lax.axis_index('row') + 1)...]
    unnamed x8 -> x20, local copies, waits for them, and re-layouts: 12.9 us -> 16.1 us
  transfers between devices with their start and end apart: 3 -> 7, of which waited for: 2 -> 6; matrix products, arithmetic and copies ran while one was open for 19% -> 21% of each run, Pallas kernels for 0% -> 0%
where the time goes in v1:
time: 290 us; the launch traced here: 286 us
  local copies, waits for them, and re-layouts  88.5 us (31%)
  waiting for transfers between devices  69.6 us (24%)
  matrix products  53.9 us (19%)
  blocking collectives  33.5 us (12%)
  other arithmetic  19.1 us (7%)
  between operations  15.1 us (5%)
  starting transfers between devices  6.5 us (2%)
    ppermute x6, waiting for transfers between devices, local(): lax.ppermute(ring[-1], 'row', [(dev, (dev + 1) % 4) for dev in range(4)])  69.6 us
    reshape x2, local copies, waits for them, and re-layouts, local(): mixed.astype(jnp.bfloat16)  27.2 us
    dot_general x2, matrix products, local(): jnp.einsum('asc,bc->asb', mixed, right_mat, preferred_element_type=jnp.fl...  23.2 us
    reshape x2, local copies, waits for them, and re-layouts, local(): contracted.astype(jnp.bfloat16)  21.5 us
    psum x2, blocking collectives, local(): lax.psum((jnp.sum(image * image), jnp.sum(image * current), jnp.sum(image...  19.4 us
    convert_element_type x2, local copies, waits for them, and re-layouts, local(): contracted.astype(jnp.bfloat16)  17.3 us
    dot_general x2, matrix products, local(): jnp.dot(left_local.reshape(rows_here * channels, bond_width), gathered.re...  16.3 us
    unnamed x20, local copies, waits for them, and re-layouts  16.1 us
  transfers between devices with their start and end apart: 7, of which 6 were waited for; matrix products, arithmetic and copies ran while one was open for 21% of the time, Pallas kernels for 0%

profile of v1, /device:TPU:0, one launch (start us, length us, event | category | flops | bytes accessed | tf_op | source)
XLA Modules:
  0.0 286.1 jit_solution(4656570897740891925)
XLA Ops:
  0.6 8.7 %copy.18 = bf16[1,512,12,512]{1,3,2,0:T(8,128)(2,1)} copy(bf16[1,512,12,512]{3,1,2,0:T(8,128)(2,1)} %param.7) | data formatting | bytes 12582912 | tf_op args[1]
  11.8 14.0 %psum.87 = f32[]{:T(128)} all-reduce(f32[]{:T(128)} %multiply_reduce_fusion.5), channel_id=1, replica_groups=mesh['seg'=8,'row'=4] {'row'}, use_global_device_ids=true, to_apply=%region_1.2 | all-reduce | flops 1 | bytes 8 | tf_op jit(solution)/shard_map/psum | solution.py:28
  27.6 14.9 %collective-permute-done = bf16[128,4,512]{2,0,1:T(8,128)(2,1)S(1)} collective-permute-done((bf16[128,4,512]{2,0,1:T(8,128)(2,1)S(1)}, bf16[128,4,512]{2,0,1:T(8,128)(2,1)S(1)}, u32[]{:S(2)}, u32[]{:S(2)}) %collective-permute-start) | collective-permute-done | bytes 524320 | tf_op jit(solution)/shard_map/ppermute | solution.py:38
  43.3 14.1 %collective-permute-done.1 = bf16[128,4,512]{2,0,1:T(8,128)(2,1)} collective-permute-done((bf16[128,4,512]{2,0,1:T(8,128)(2,1)S(1)}, bf16[128,4,512]{2,0,1:T(8,128)(2,1)}, u32[]{:S(2)}, u32[]{:S(2)}) %collective-permute-start.1) | collective-permute-done | bytes 524320 | tf_op jit(solution)/shard_map/ppermute | solution.py:38
  61.4 9.3 %collective-permute-done.2 = bf16[128,4,512]{2,0,1:T(8,128)(2,1)} collective-permute-done((bf16[128,4,512]{2,0,1:T(8,128)(2,1)}, bf16[128,4,512]{2,0,1:T(8,128)(2,1)}, u32[]{:S(2)}, u32[]{:S(2)}) %collective-permute-start.2) | collective-permute-done | bytes 524320 | tf_op jit(solution)/shard_map/ppermute | solution.py:38
  70.7 4.6 %fusion.16 = bf16[512,4,512]{2,0,1:T(8,128)(2,1)S(1)} fusion(s32[]{:T(128)S(6)} %select_n.23, bf16[128,4,512]{2,0,1:T(8,128)(2,1)} %collective-permute-done.2, bf16[128,4,512]{2,0,1:T(8,128)(2,1)} %collective-permute-done.1, bf16[128,4,512]{2,0,1:T(8,128)(2,1)} %copy-done.4, bf16[128,4,512]{2,0,1:T(8,128)(2,1)} %copy-done.2), kind=kLoop, calls=%fused_computation.37 | loop fusion | flops 16777216 | bytes 4194308 | tf_op jit(solution)/shard_map/jit(_roll_dynamic)/concatenate | solution.py:39
  77.7 8.1 %fusion = bf16[1536,2048]{0,1:T(8,128)(2,1)} fusion(bf16[512,2048]{0,1:T(8,128)(2,1)} %bitcast.73, bf16[1536,512]{1,0:T(8,128)(2,1)} %reshape_squeeze.7), kind=kOutput, calls=%fused_computation.2 | convolution fusion | flops 3224371200 | bytes 9961472 | tf_op jit(solution)/shard_map/dot_general | solution.py:44
  85.8 8.7 %copy.14 = bf16[1536,2048]{1,0:T(8,128)(2,1)} copy(bf16[1536,2048]{0,1:T(8,128)(2,1)} %fusion) | data formatting | bytes 12582912 | tf_op jit(solution)/shard_map/convert_element_type | solution.py:49
  94.5 10.8 %reshape.37 = bf16[128,48,512]{2,1,0:T(8,128)(2,1)} reshape(bf16[1536,2048]{1,0:T(8,128)(2,1)} %copy.14) | data formatting | bytes 12582912 | tf_op jit(solution)/shard_map/reshape | solution.py:49
  105.2 7.2 %convert_bitcast_fusion.1 = bf16[128,48,512]{2,1,0:T(8,128)(2,1)} fusion(bf16[128,48,512]{2,1,0:T(8,128)(2,1)} %reshape.37, bf16[48,48]{0,1:T(8,128)(2,1)S(1)} %reshape.38), kind=kOutput, calls=%fused_computation.9 | convolution fusion | flops 305135616 | bytes 12587520 | tf_op jit(solution)/shard_map/ik,akb->aib/dot_general | solution.py:52
  112.4 13.6 %reshape.39 = bf16[128,4,6144]{2,1,0:T(4,128)(2,1)} reshape(bf16[128,48,512]{2,1,0:T(8,128)(2,1)} %convert_bitcast_fusion.1) | data formatting | bytes 12582912 | tf_op jit(solution)/shard_map/reshape | solution.py:55
  126.0 6.1 %broadcast_select_fusion = bf16[1,512,12,512]{1,3,2,0:T(8,128)(2,1)} fusion(bf16[1,512,12,512]{1,3,2,0:T(8,128)(2,1)} %copy.18, bf16[1,512,12,512]{1,3,2,0:T(8,128)(2,1)} %collective-permute-done.3, pred[]{:T(512)S(6)} %eq.5), kind=kLoop, calls=%fused_computation.10 | loop fusion | flops 3145728 | bytes 18874368 | tf_op jit(solution)/shard_map/jit(_where)/select_n | solution.py:25
  132.1 11.5 %fusion.24 = (f32[]{:T(128)}, f32[]{:T(128)}, f32[]{:T(128)}, f32[]{:T(128)}, f32[]{:T(128)}, /*index=5*/f32[128,4,512]{2,0,1:T(8,128)S(1)}) fusion(f32[]{:T(128)S(6)} %sqrt.9, f32[1,128,4,512]{3,2,1,0:T(4,128)S(1)} %copy-done, bf16[512,6144,1]{0,1,2:T(8,128)(2,1)} %bitcast.70, bf16[128,4,6144]{2,1,0:T(4,128)(2,1)} %reshape.39), kind=kOutput, calls=%fused_computation.53 | convolution fusion | flops 3224109056 | bytes 14680088 | tf_op jit(solution)/shard_map/asc,bc->asb/dot_general | solution.py:56
  143.6 9.6 %all-reduce.1 = (f32[]{:T(128)}, f32[]{:T(128)}, f32[]{:T(128)}, f32[]{:T(128)}, f32[]{:T(128)}, /*index=5*/f32[]{:T(128)}) all-reduce(f32[]{:T(128)} %get-tuple-element.19, f32[]{:T(128)} %get-tuple-element.17, f32[]{:T(128)} %get-tuple-element.18, f32[]{:T(128)} %get-tuple-element.16, ...), channel_id=1, replica_groups=mesh['seg'=8,'row'=4] {'row'}, use_global_device_ids=true, to_apply=%region_5.7 | all-reduce | flops 6 | bytes 48 | tf_op jit(solution)/shard_map/psum | solution.py:57
  164.4 10.2 %collective-permute-done.4 = bf16[128,4,512]{2,0,1:T(8,128)(2,1)S(1)} collective-permute-done((bf16[128,4,512]{2,0,1:T(8,128)(2,1)S(1)}, bf16[128,4,512]{2,0,1:T(8,128)(2,1)S(1)}, u32[]{:S(2)}, u32[]{:S(2)}) %collective-permute-start.4) | collective-permute-done | bytes 524320 | tf_op jit(solution)/shard_map/ppermute | solution.py:38
  177.2 12.3 %collective-permute-done.5 = bf16[128,4,512]{2,0,1:T(8,128)(2,1)S(1)} collective-permute-done((bf16[128,4,512]{2,0,1:T(8,128)(2,1)S(1)}, bf16[128,4,512]{2,0,1:T(8,128)(2,1)S(1)}, u32[]{:S(2)}, u32[]{:S(2)}) %collective-permute-start.5) | collective-permute-done | bytes 524320 | tf_op jit(solution)/shard_map/ppermute | solution.py:38
  191.7 8.9 %collective-permute-done.6 = bf16[128,4,512]{2,0,1:T(8,128)(2,1)} collective-permute-done((bf16[128,4,512]{2,0,1:T(8,128)(2,1)S(1)}, bf16[128,4,512]{2,0,1:T(8,128)(2,1)}, u32[]{:S(2)}, u32[]{:S(2)}) %collective-permute-start.6) | collective-permute-done | bytes 524320 | tf_op jit(solution)/shard_map/ppermute | solution.py:38
  207.6 8.2 %fusion.1 = bf16[1536,2048]{0,1:T(8,128)(2,1)} fusion(bf16[512,2048]{0,1:T(8,128)(2,1)} %bitcast.72, bf16[1536,512]{1,0:T(8,128)(2,1)} %reshape_squeeze.7), kind=kOutput, calls=%fused_computation.3 | convolution fusion | flops 3224371200 | bytes 9961472 | tf_op jit(solution)/shard_map/dot_general | solution.py:44
  215.7 8.6 %copy.22 = bf16[1536,2048]{1,0:T(8,128)(2,1)} copy(bf16[1536,2048]{0,1:T(8,128)(2,1)} %fusion.1) | data formatting | bytes 12582912 | tf_op jit(solution)/shard_map/convert_element_type | solution.py:49
  224.4 10.7 %reshape.41 = bf16[128,48,512]{2,1,0:T(8,128)(2,1)} reshape(bf16[1536,2048]{1,0:T(8,128)(2,1)} %copy.22) | data formatting | bytes 12582912 | tf_op jit(solution)/shard_map/reshape | solution.py:49
  235.1 7.2 %convert_bitcast_fusion = bf16[128,48,512]{2,1,0:T(8,128)(2,1)} fusion(bf16[128,48,512]{2,1,0:T(8,128)(2,1)} %reshape.41, bf16[48,48]{0,1:T(8,128)(2,1)S(1)} %reshape.38), kind=kOutput, calls=%fused_computation.8 | convolution fusion | flops 305135616 | bytes 12587520 | tf_op jit(solution)/shard_map/ik,akb->aib/dot_general | solution.py:52
  242.3 13.7 %reshape.42 = bf16[128,4,6144]{2,1,0:T(4,128)(2,1)} reshape(bf16[128,48,512]{2,1,0:T(8,128)(2,1)} %convert_bitcast_fusion) | data formatting | bytes 12582912 | tf_op jit(solution)/shard_map/reshape | solution.py:55
  256.0 11.7 %fusion.29 = (f32[]{:T(128)}, f32[]{:T(128)}, f32[]{:T(128)}, f32[]{:T(128)}, f32[]{:T(128)}, /*index=5*/f32[128,4,512]{2,0,1:T(8,128)S(1)}) fusion(f32[128,4,512]{2,0,1:T(8,128)S(1)} %copy-done.1, f32[]{:T(128)S(6)} %sqrt.9, f32[1,128,4,512]{3,2,1,0:T(4,128)S(1)} %copy-done, bf16[512,6144,1]{0,1,2:T(8,128)(2,1)} %bitcast.71, bf16[128,4,6144]{2,1,0:T(4,128)(2,1)} %reshape.42), kind=kOutput, calls=%fused_computation.58 | convolution fusion | flops 3224109056 | bytes 15728664 | tf_op jit(solution)/shard_map/asc,bc->asb/dot_general | solution.py:56
  267.7 9.8 %all-reduce = (f32[]{:T(128)}, f32[]{:T(128)}, f32[]{:T(128)}, f32[]{:T(128)}, f32[]{:T(128)}) all-reduce(f32[]{:T(128)} %get-tuple-element.13, f32[]{:T(128)} %get-tuple-element.12, f32[]{:T(128)} %get-tuple-element.11, f32[]{:T(128)} %get-tuple-element.14, f32[]{:T(128)} %get-tuple-element.10), channel_id=1, replica_groups=mesh['seg'=8,'row'=4] {'row'}, use_global_device_ids=true, to_apply=%region_16.18 | all-reduce | flops 5 | bytes 40 | tf_op jit(solution)/shard_map/psum | solution.py:57
  (37 shorter events, 28.7 us)
Async XLA Ops:
  0.6 10.0 %copy-start = (f32[1,128,4,512]{3,2,1,0:T(4,128)S(1)}, f32[1,128,4,512]{3,2,1,0:T(4,128)}, u32[]{:S(2)}) copy-start(f32[1,128,4,512]{3,2,1,0:T(4,128)} %param.9) | copy-start | bytes 3145732
  9.4 116.7 %collective-permute-start.3 = (bf16[1,512,12,512]{1,3,2,0:T(8,128)(2,1)}, bf16[1,512,12,512]{1,3,2,0:T(8,128)(2,1)}, u32[]{:S(2)}, u32[]{:S(2)}) collective-permute-start(bf16[1,512,12,512]{1,3,2,0:T(8,128)(2,1)} %copy.18), channel_id=1, source_target_pairs={{4,0},{8,4},{12,8},{16,12},{20,16},{24,20},{28,24},{5,1},{9,5},{13... | collective-permute-start | bytes 18874376 | tf_op jit(solution)/shard_map/ppermute | solution.py:12
  26.5 34.6 %copy-start.7 = (bf16[4,12,12,4]{2,3,1,0:T(4,128)(2,1)S(1)}, bf16[4,12,12,4]{2,3,1,0:T(4,128)(2,1)}, u32[]{:S(2)}) copy-start(bf16[4,12,12,4]{2,3,1,0:T(4,128)(2,1)} %param.8) | copy-start | bytes 13828
  26.8 0.8 copy-start.2
  27.6 14.9 %collective-permute-start = (bf16[128,4,512]{2,0,1:T(8,128)(2,1)S(1)}, bf16[128,4,512]{2,0,1:T(8,128)(2,1)S(1)}, u32[]{:S(2)}, u32[]{:S(2)}) collective-permute-start(bf16[128,4,512]{2,0,1:T(8,128)(2,1)S(1)} %bitcast_convert_fusion), channel_id=1, source_target_pairs={{0,1},{1,2},{2,3},{3,0},{4,5},{5,6},{6,7},{7,4},{8,9},{9,10},{10,1... | collective-permute-start | bytes 1572872 | tf_op jit(solution)/shard_map/ppermute | solution.py:38
  42.5 0.8 copy-start.4
  43.3 14.1 %collective-permute-start.1 = (bf16[128,4,512]{2,0,1:T(8,128)(2,1)S(1)}, bf16[128,4,512]{2,0,1:T(8,128)(2,1)}, u32[]{:S(2)}, u32[]{:S(2)}) collective-permute-start(bf16[128,4,512]{2,0,1:T(8,128)(2,1)S(1)} %collective-permute-done), channel_id=1, source_target_pairs={{0,1},{1,2},{2,3},{3,0},{4,5},{5,6},{6,7},{7,4},{8,9},{9,10},{10,1... | collective-permute-start | bytes 1572872 | tf_op jit(solution)/shard_map/ppermute | solution.py:38
  57.3 13.3 %collective-permute-start.2 = (bf16[128,4,512]{2,0,1:T(8,128)(2,1)}, bf16[128,4,512]{2,0,1:T(8,128)(2,1)}, u32[]{:S(2)}, u32[]{:S(2)}) collective-permute-start(bf16[128,4,512]{2,0,1:T(8,128)(2,1)} %collective-permute-done.1), channel_id=1, source_target_pairs={{0,1},{1,2},{2,3},{3,0},{4,5},{5,6},{6,7},{7,4},{8,9},{9,10},{10,1... | collective-permute-start | bytes 1572872 | tf_op jit(solution)/shard_map/ppermute | solution.py:38
  161.6 0.8 copy-start.3
  162.5 12.2 %collective-permute-start.4 = (bf16[128,4,512]{2,0,1:T(8,128)(2,1)S(1)}, bf16[128,4,512]{2,0,1:T(8,128)(2,1)S(1)}, u32[]{:S(2)}, u32[]{:S(2)}) collective-permute-start(bf16[128,4,512]{2,0,1:T(8,128)(2,1)S(1)} %get-tuple-element.31), channel_id=1, source_target_pairs={{0,1},{1,2},{2,3},{3,0},{4,5},{5,6},{6,7},{7,4},{8,9},{9,10},{10,1... | collective-permute-start | bytes 1572872 | tf_op jit(solution)/shard_map/ppermute | solution.py:38
  174.6 0.8 copy-start.5
  175.4 14.1 %collective-permute-start.5 = (bf16[128,4,512]{2,0,1:T(8,128)(2,1)S(1)}, bf16[128,4,512]{2,0,1:T(8,128)(2,1)S(1)}, u32[]{:S(2)}, u32[]{:S(2)}) collective-permute-start(bf16[128,4,512]{2,0,1:T(8,128)(2,1)S(1)} %collective-permute-done.4), channel_id=1, source_target_pairs={{0,1},{1,2},{2,3},{3,0},{4,5},{5,6},{6,7},{7,4},{8,9},{9,10},{10,1... | collective-permute-start | bytes 1572872 | tf_op jit(solution)/shard_map/ppermute | solution.py:38
  189.5 2.2 copy-start.6
  189.5 11.1 %collective-permute-start.6 = (bf16[128,4,512]{2,0,1:T(8,128)(2,1)S(1)}, bf16[128,4,512]{2,0,1:T(8,128)(2,1)}, u32[]{:S(2)}, u32[]{:S(2)}) collective-permute-start(bf16[128,4,512]{2,0,1:T(8,128)(2,1)S(1)} %collective-permute-done.5), channel_id=1, source_target_pairs={{0,1},{1,2},{2,3},{3,0},{4,5},{5,6},{6,7},{7,4},{8,9},{9,10},{10,1... | collective-permute-start | bytes 1572872 | tf_op jit(solution)/shard_map/ppermute | solution.py:38
  242.3 13.7 %copy-start.1 = (f32[128,4,512]{2,0,1:T(8,128)S(1)}, f32[128,4,512]{2,0,1:T(8,128)}, u32[]{:S(2)}) copy-start(f32[128,4,512]{2,0,1:T(8,128)} %get-tuple-element.32) | copy-start | bytes 3145732
